TPU v7x, 32 devices: a whole 2x2x4 slice. The times are simulated.
32 devices in a mesh: tm: 8 (over z, y), space: 4 (over x, core).
Axes of the slice: x: 2, y: 2, z: 4, core: 2. Of those that a mesh axis runs over, the one named last changes fastest.
Arguments:
- snapshots: bfloat16 [4096, 3, 4096], P('tm', None, 'space'), may hold values from -6 to 6
- cell_weights: float32 [4096], P('space'), may hold values from 0.25 to 4
- triads: int32 [64, 3], replicated, may hold values from 0 to 127, as said below
- owner_slots: int32 [8, 16], replicated, may hold values from -1 to 63, as said below
Outputs:
- bispectra: float32 [128, 512], P(('tm', 'space'))
Inputs may be any that keep to these rules, and one draw needn't show every extreme that they name: `triads`: every row is (k, l, k + l); all three entries are below 128. `owner_slots`: every triad index stands in exactly one slot of the table; in each row the used slots come first and the others hold -1; some owner fills all 16 slots.
All inputs are finite; a program needn't handle non-finite values.
Results may differ from a plain program's by a relative error of at most 0.0076.
Values may be sent and summed in bfloat16 or wider, within the bound.
A program may use at most 64 MiB of HBM per device.

v0:
```python
import functools
import math

import jax
import jax.numpy as jnp
import ml_dtypes
import numpy as np
from jax import lax
from jax.experimental import pallas as pl
from jax.experimental.pallas import tpu as pltpu
from jax.sharding import PartitionSpec as P

NB = 16
NT = 256
K = 128
GROUP = 8
LANES = 128
MESH = pl.DeviceIdType.MESH


def spectral_table():
    sample = np.arange(NT)
    freq_bins = np.arange(K)
    angles = 2.0 * math.pi / NT * (freq_bins[:, None] * sample[None, :] % NT)
    window = 0.5 - 0.5 * np.cos(2.0 * math.pi / NT * sample)
    scale = math.sqrt(8.0 / (3.0 * NT))
    rows = np.stack(
        [scale * window * np.cos(angles), -scale * window * np.sin(angles)], axis=1
    )
    return rows.reshape(2 * K, NT).astype(np.float32).astype(ml_dtypes.bfloat16)


def kernel(
    n,
    ns,
    weight_scale,
    snap,
    table,
    weights,
    freqs,
    out,
    recv,
    rows,
    spec,
    narrow,
    acc,
    part,
    summed,
    last,
    send_sem,
    recv_sem,
    own_sem,
    send1,
    recv1,
    send2,
    recv2,
):
    comps, times = snap.shape[0], snap.shape[1]
    me = lax.axis_index("tm")
    col = lax.axis_index("space")

    barrier = pltpu.get_barrier_semaphore()

    def greet_tm(off, carry):
        pl.semaphore_signal(
            barrier, inc=1, device_id=(lax.rem(me + off, n), col), device_id_type=MESH
        )
        return carry

    lax.fori_loop(1, n, greet_tm, 0)
    for off in range(1, ns):
        pl.semaphore_signal(
            barrier, inc=1, device_id=(me, lax.rem(col + off, ns)), device_id_type=MESH
        )
    pl.semaphore_wait(barrier, n - 1 + ns - 1)

    def exchange(c, off):
        peer = lax.rem(me + off, n)
        return pltpu.make_async_remote_copy(
            src_ref=snap.at[c, :, pl.ds(pl.multiple_of(peer * LANES, LANES), LANES)],
            dst_ref=recv.at[c, pl.ds(pl.multiple_of(me * times, 16), times), :],
            send_sem=send_sem.at[c, off],
            recv_sem=recv_sem.at[c, off],
            device_id=(peer, col),
            device_id_type=MESH,
        )

    def own(c):
        return pltpu.make_async_copy(
            snap.at[c, :, pl.ds(pl.multiple_of(me * LANES, LANES), LANES)],
            recv.at[c, pl.ds(pl.multiple_of(me * times, 16), times), :],
            own_sem.at[c],
        )

    for c in range(comps):

        def begin(off, carry, c=c):
            exchange(c, off).start()
            return carry

        lax.fori_loop(1, n, begin, 0)
        own(c).start()

    w_row = weights[pl.ds(me, 1), :] * weight_scale
    lane = lax.broadcasted_iota(jnp.int32, (2 * NB, 2 * LANES), 1)
    lane_group = lax.rem(lane, LANES) // NB
    low = lax.broadcasted_iota(jnp.int32, (NB, LANES), 1) < LANES // 2
    groups = freqs.shape[1] // GROUP
    per_owner = groups // n

    def dft(c, b):
        x = recv[c, pl.ds(pl.multiple_of(b * NT, NT), NT), :]
        y = jnp.dot(table[...], x, preferred_element_type=jnp.float32)
        rows[pl.ds(b, 2 * K, stride=NB), :] = y

    def regroup(k, carry):
        both = rows[pl.ds(pl.multiple_of(k * 2 * NB, 2 * NB), 2 * NB), :].astype(jnp.bfloat16)
        narrow[k] = both
        spec[k] = both.astype(jnp.float32)
        return carry

    def gram_group(c, g):
        owner = g // per_owner
        half = lax.rem(g, per_owner)
        prods, c_re, c_im = [], [], []
        for s in range(GROUP):
            place = g * GROUP + s
            a = spec[freqs[0, place]]
            b2 = spec[freqs[1, place]]
            c2 = narrow[freqs[2, place]]
            re = (a[:NB] * b2[:NB] - a[NB:] * b2[NB:]) * w_row
            im = (a[:NB] * b2[NB:] + a[NB:] * b2[:NB]) * w_row
            prods += [re.astype(jnp.bfloat16), im.astype(jnp.bfloat16)]
            c_re.append(c2[:NB])
            c_im.append(c2[NB:])
        left = jnp.concatenate(prods, axis=0)
        right = jnp.concatenate(c_re + c_im, axis=0)
        gram = lax.dot_general(
            left, right, (((1,), (1,)), ((), ())), preferred_element_type=jnp.float32
        )
        diag = gram[: 2 * NB]
        for s in range(1, GROUP):
            diag = jnp.where(lane_group == s, gram[2 * NB * s : 2 * NB * (s + 1)], diag)
        real = diag[:NB, :LANES] + diag[NB:, LANES:]
        imag = diag[:NB, LANES:] - diag[NB:, :LANES]
        half_turn = LANES // 2
        first = jnp.where(low, real, pltpu.roll(imag, half_turn, 1))
        second = jnp.where(low, pltpu.roll(real, half_turn, 1), imag)
        if c == 0:
            acc[2 * half, owner] = first
            acc[2 * half + 1, owner] = second
        else:
            acc[2 * half, owner] += first
            acc[2 * half + 1, owner] += second

    for c in range(comps):
        own(c).wait()
        if times % NT == 0:

            def transform(i, carry, c=c):
                dft(c, me * (times // NT) + i)
                return carry

            lax.fori_loop(0, times // NT, transform, 0)

            def arrive(off, carry, c=c):
                exchange(c, off).wait_recv()
                src = lax.rem(me - off + n, n)
                for i in range(times // NT):
                    dft(c, src * (times // NT) + i)
                return carry

            lax.fori_loop(1, n, arrive, 0)
        else:

            def arrive(off, carry, c=c):
                exchange(c, off).wait_recv()
                return carry

            lax.fori_loop(1, n, arrive, 0)

            def transform(b, carry, c=c):
                dft(c, b)
                return carry

            lax.fori_loop(0, NB, transform, 0)

        lax.fori_loop(0, K, regroup, 0, unroll=4)

        def grams(g, carry, c=c):
            gram_group(c, g)
            return carry

        lax.fori_loop(0, groups, grams, 0)

    def across(off):
        peer = lax.rem(col + off, ns)
        return pltpu.make_async_remote_copy(
            src_ref=acc.at[peer],
            dst_ref=part.at[off - 1],
            send_sem=send1.at[off - 1],
            recv_sem=recv1.at[off - 1],
            device_id=(me, peer),
            device_id_type=MESH,
        )

    for off in range(1, ns):
        across(off).start()
    for off in range(1, ns):
        across(off).wait_recv()
    total = acc[col]
    for off in range(1, ns):
        total = total + part[off - 1]
    summed[...] = total

    def along(off):
        peer = lax.rem(me + off, n)
        return pltpu.make_async_remote_copy(
            src_ref=summed.at[peer],
            dst_ref=last.at[off],
            send_sem=send2.at[off],
            recv_sem=recv2.at[off],
            device_id=(peer, col),
            device_id_type=MESH,
        )

    def begin2(off, carry):
        along(off).start()
        return carry

    lax.fori_loop(1, n, begin2, 0)

    def add2(off, total):
        along(off).wait_recv()
        return total + last[off]

    out[...] = lax.fori_loop(1, n, add2, summed[me])

    for off in range(1, ns):
        across(off).wait_send()

    def drain(off, carry):
        for c in range(comps):
            exchange(c, off).wait_send()
        along(off).wait_send()
        return carry

    lax.fori_loop(1, n, drain, 0)


def shards(n, ns, snapshots, cell_weights, triads, owner_slots):
    times, comps, cells = snapshots.shape
    owners, slot_count = owner_slots.shape
    weight_scale = 1.0 / math.sqrt(comps * cells * ns)
    vmem = pl.BlockSpec(memory_space=pltpu.VMEM)
    smem = pl.BlockSpec(memory_space=pltpu.SMEM)
    anywhere = pl.BlockSpec(memory_space=pl.ANY)
    sem = pltpu.SemaphoreType.DMA
    tile = pl.pallas_call(
        functools.partial(kernel, n, ns, weight_scale),
        out_shape=jax.ShapeDtypeStruct((NB, LANES), jnp.float32),
        in_specs=[anywhere, vmem, vmem, smem],
        out_specs=vmem,
        scratch_shapes=[
            pltpu.VMEM((comps, NB * NT, LANES), jnp.bfloat16),
            pltpu.VMEM((2 * K * NB, LANES), jnp.float32),
            pltpu.VMEM((K, 2 * NB, LANES), jnp.float32),
            pltpu.VMEM((K, 2 * NB, LANES), jnp.bfloat16),
            pltpu.VMEM((ns, n, NB, LANES), jnp.float32),
            pltpu.VMEM((ns - 1, n, NB, LANES), jnp.float32),
            pltpu.VMEM((n, NB, LANES), jnp.float32),
            pltpu.VMEM((n, NB, LANES), jnp.float32),
            sem((comps, n)),
            sem((comps, n)),
            sem((comps,)),
            sem((ns - 1,)),
            sem((ns - 1,)),
            sem((n,)),
            sem((n,)),
        ],
        compiler_params=pltpu.CompilerParams(
            collective_id=0, has_side_effects=True, vmem_limit_bytes=40 * 1024 * 1024
        ),
    )(
        snapshots.transpose(1, 0, 2),
        jnp.asarray(spectral_table()),
        cell_weights.reshape(n, LANES),
        jnp.take(triads.T, jnp.maximum(owner_slots, 0).reshape(-1), axis=1, mode="clip"),
    )
    mine = slot_count // ns
    flat = tile.reshape(NB, 2, mine, NB).transpose(2, 1, 0, 3).reshape(mine, 2 * NB * NB)
    my_slots = lax.dynamic_slice(
        owner_slots, (lax.axis_index("tm"), lax.axis_index("space") * mine), (1, mine)
    ).reshape(mine, 1)
    return jnp.where(my_slots >= 0, flat, 0.0)


def solution(mesh):
    placed = (P("tm", None, "space"), P("space"), P(), P())
    n, ns = mesh.shape["tm"], mesh.shape["space"]
    return jax.shard_map(
        functools.partial(shards, n, ns),
        mesh=mesh,
        in_specs=placed,
        out_specs=P(("tm", "space"), None),
        check_vma=False,
    )
```

profile of v0, /device:TPU:0, one launch (start us, length us, event | category | flops | bytes accessed | tf_op | source)
XLA Modules:
  0.0 97.1 jit_solution(9721842767064481788)
XLA Ops:
  0.0 0.8 copy.6
  0.8 0.7 broadcast_maximum_fusion
  1.5 0.1 reshape.26
  1.6 0.6 gather_fusion
  2.2 0.1 copy.7
  2.3 0.0 copy-start
  2.3 1.9 %copy-done = bf16[512,3,1024]{2,0,1:T(8,128)(2,1)S(1)} copy-done((bf16[512,3,1024]{2,0,1:T(8,128)(2,1)S(1)}, bf16[512,3,1024]{2,0,1:T(8,128)(2,1)}, u32[]{:S(2)}) %copy-start) | copy-done | bytes 3145752
  4.2 0.0 copy-start.1
  4.2 0.9 copy-done.1
  5.1 0.0 copy-start.2
  5.1 0.7 copy-done.2
  5.8 89.7 %shard_map.55 = f32[16,128]{1,0:T(8,128)S(1)} custom-call(bf16[3,512,1024]{2,1,0:T(8,128)(2,1)S(1)} %bitcast.9, bf16[256,256]{1,0:T(8,128)(2,1)S(1)} %copy-done.1, f32[8,128]{1,0:T(8,128)S(1)} %bitcast.11, s32[3,128]{1,0:T(4,128)S(1)} %bitcast.10), custom_call_target="tpu_custom_call" | custom-call | tf_op jit(solution)/shard_map/pallas_call | solution.py:259
  95.5 0.1 reshape.22
  95.6 0.1 reshape.23
  95.7 0.8 compare_bitcast_fusion
  96.5 0.7 broadcast_select_fusion
  (2 shorter events, 0.0 us)
Async XLA Ops:
  2.3 1.9 %copy-start = (bf16[512,3,1024]{2,0,1:T(8,128)(2,1)S(1)}, bf16[512,3,1024]{2,0,1:T(8,128)(2,1)}, u32[]{:S(2)}) copy-start(bf16[512,3,1024]{2,0,1:T(8,128)(2,1)} %param.5) | copy-start | bytes 9437188
  4.2 0.9 copy-start.1
  5.1 0.7 copy-start.2
where the time goes:
time: 97.4 us; the launch traced here: 97.1 us
  Pallas kernels  89.7 us (92%)
  local copies, waits for them, and re-layouts  5.27 us (5%)
  other arithmetic  2.14 us (2%)
    pallas_call x1, Pallas kernels, shards(): pl.pallas_call(functools.partial(kernel, n, ns, weight_scale), out_shape=...  89.7 us
    unnamed x7, local copies, waits for them, and re-layouts  4.27 us

commit v1 on v0

--- a/solution.py
+++ b/solution.py
@@ -248,9 +248,411 @@
     lax.fori_loop(1, n, drain, 0)
 
 
+def lean_kernel(
+    n,
+    ns,
+    bins,
+    weight_scale,
+    snap,
+    table,
+    weights,
+    triads,
+    slots,
+    out,
+    series,
+    tab,
+    dft,
+    pick,
+    stage,
+    recv,
+    looked,
+    prod,
+    third,
+    acc,
+    tiles,
+    part,
+    summed,
+    last,
+    load_sem,
+    send_sem,
+    recv_sem,
+    send1,
+    recv1,
+    send2,
+    recv2,
+):
+    comps, times, cells = series.shape
+    blocks = times // NT
+    count = triads.shape[1]
+    owners, per_owner = slots.shape
+    total_slots = owners * per_owner
+    groups = total_slots // GROUP
+    halves = per_owner // GROUP
+    me = lax.axis_index("tm")
+    col = lax.axis_index("space")
+    f32, bf16 = jnp.float32, jnp.bfloat16
+
+    def iota(shape, axis):
+        return lax.broadcasted_iota(jnp.int32, shape, axis)
+
+    fetch_table = pltpu.make_async_copy(table, tab, load_sem.at[comps])
+    fetch_table.start()
+
+    def fetch(c):
+        return pltpu.make_async_copy(snap.at[c], series.at[c], load_sem.at[c])
+
+    for c in range(comps):
+        fetch(c).start()
+
+    barrier = pltpu.get_barrier_semaphore()
+
+    def greet(off, carry):
+        pl.semaphore_signal(
+            barrier, inc=1, device_id=(lax.rem(me + off, n), col), device_id_type=MESH
+        )
+        return carry
+
+    lax.fori_loop(1, n, greet, 0)
+    for off in range(1, ns):
+        pl.semaphore_signal(
+            barrier, inc=1, device_id=(me, lax.rem(col + off, ns)), device_id_type=MESH
+        )
+
+    freq = iota((K, count), 0)
+    hit = (
+        (freq == triads[0:1, :]) | (freq == triads[1:2, :]) | (freq == triads[2:3, :])
+    )
+    used = jnp.max(jnp.where(hit, 1.0, 0.0), axis=1, keepdims=True)
+    used = jnp.broadcast_to(used, (K, K))
+    column = iota((K, K), 1)
+    below = jnp.where(column < iota((K, K), 0), 1.0, 0.0)
+    rank = jnp.dot(below.astype(bf16), used.astype(bf16), preferred_element_type=f32)
+    place = jnp.where((rank == column.astype(f32)) & (used > 0.0), 1.0, 0.0)
+    chosen = place.T[:bins].astype(bf16)
+    fetch_table.wait()
+    dft[...] = jnp.concatenate(
+        [jnp.dot(chosen, tab[r], preferred_element_type=f32) for r in range(2)], axis=0
+    ).astype(bf16)
+
+    def transform(c):
+        fetch(c).wait()
+
+        def step(p, carry):
+            for b in range(blocks):
+                y = jnp.dot(
+                    dft[...],
+                    series[
+                        c,
+                        b * NT : (b + 1) * NT,
+                        pl.ds(pl.multiple_of(p * 2 * LANES, 2 * LANES), 2 * LANES),
+                    ],
+                    preferred_element_type=f32,
+                ).astype(bf16)
+                rows = pl.ds(b * 2 * bins, 2 * bins)
+                stage[c, 2 * p, rows, :] = y[:, :LANES]
+                stage[c, 2 * p + 1, rows, :] = y[:, LANES:]
+            return carry
+
+        lax.fori_loop(0, n // 2, step, 0)
+
+    def exchange(c, off):
+        peer = lax.rem(me + off, n)
+        return pltpu.make_async_remote_copy(
+            src_ref=stage.at[c, peer],
+            dst_ref=recv.at[c, me],
+            send_sem=send_sem.at[c, off],
+            recv_sem=recv_sem.at[c, off],
+            device_id=(peer, col),
+            device_id_type=MESH,
+        )
+
+    transform(0)
+    pl.semaphore_wait(barrier, n - 1 + ns - 1)
+    for c in range(comps):
+        if c > 0:
+            transform(c)
+
+        def begin(off, carry, c=c):
+            exchange(c, off).start()
+            return carry
+
+        lax.fori_loop(1, n, begin, 0)
+
+    wide = (owners, total_slots)
+    spread = jnp.where(
+        lax.rem(iota((per_owner, total_slots), 1), per_owner)
+        == iota((per_owner, total_slots), 0),
+        1.0,
+        0.0,
+    )
+    tiled = jnp.dot(
+        slots[...].astype(f32).astype(bf16),
+        spread.astype(bf16),
+        preferred_element_type=f32,
+    )
+    own_row = iota(wide, 1) // per_owner == iota(wide, 0)
+    slot_triad = jnp.sum(jnp.where(own_row, tiled, 0.0), axis=0, keepdims=True)
+    holds = jnp.where(
+        iota((count, total_slots), 0).astype(f32) == slot_triad, 1.0, 0.0
+    ).astype(bf16)
+    slot_freq = jnp.dot(
+        (triads[...] + 1).astype(f32).astype(bf16), holds, preferred_element_type=f32
+    )
+    for role in range(3):
+        named = jnp.where(
+            iota((K, total_slots), 0).astype(f32) + 1.0 == slot_freq[role : role + 1, :],
+            1.0,
+            0.0,
+        )
+        chosen_all = jnp.dot(
+            place.T.astype(bf16), named.astype(bf16), preferred_element_type=f32
+        )
+        pick[role * total_slots : (role + 1) * total_slots, :] = chosen_all.T[
+            :, :bins
+        ].astype(bf16)
+
+    w_row = weights[pl.ds(me, 1), :] * weight_scale
+
+    def look_up(c, src, ref):
+        for pair in range(blocks // 2):
+            sides = []
+            for b in (2 * pair, 2 * pair + 1):
+                both = ref[c, src, b * 2 * bins : (b + 1) * 2 * bins, :]
+                if bins % 16 != 0:
+                    both = both.astype(f32)
+                sides += [both[:bins], both[bins:]]
+            looked[...] = jnp.dot(
+                pick[...],
+                jnp.concatenate(sides, axis=1).astype(bf16),
+                preferred_element_type=f32,
+            )
+            first = src * (blocks * GROUP) + pair * 2 * GROUP
+            at = pl.ds(pl.multiple_of(first, 2 * GROUP), 2 * GROUP)
+            at_imag = pl.ds(pl.multiple_of(NB * GROUP + first, 2 * GROUP), 2 * GROUP)
+
+            def group(g, carry):
+                def tile(role, q):
+                    row = pl.multiple_of(role * total_slots + g * GROUP, GROUP)
+                    return looked[pl.ds(row, GROUP), q * LANES : (q + 1) * LANES]
+
+                re, im, c_re, c_im = [], [], [], []
+                for b in range(2):
+                    ar, ai = tile(0, 2 * b), tile(0, 2 * b + 1)
+                    br, bi = tile(1, 2 * b), tile(1, 2 * b + 1)
+                    re.append((ar * br - ai * bi) * w_row)
+                    im.append((ar * bi + ai * br) * w_row)
+                    c_re.append(tile(2, 2 * b))
+                    c_im.append(tile(2, 2 * b + 1))
+                re, im, c_re, c_im = (
+                    jnp.concatenate(v, axis=0) for v in (re, im, c_re, c_im)
+                )
+                prod[g, at, :LANES] = re.astype(bf16)
+                prod[g, at, LANES:] = im.astype(bf16)
+                third[g, at, :LANES] = c_re.astype(bf16)
+                third[g, at, LANES:] = c_im.astype(bf16)
+                third[g, at_imag, :LANES] = c_im.astype(bf16)
+                third[g, at_imag, LANES:] = (-c_re).astype(bf16)
+                return carry
+
+            lax.fori_loop(0, groups, group, 0, unroll=4)
+
+    def gram(g):
+        return lax.dot_general(
+            prod[g], third[g], (((1,), (1,)), ((), ())), preferred_element_type=f32
+        )
+
+    sub = iota((GROUP, LANES), 0)
+    keep = sub == lax.rem(iota((GROUP, LANES), 1), GROUP)
+    low = lax.rem(iota((NB, LANES), 1), GROUP) < GROUP // 2
+
+    def diagonal(total, side):
+        octets = []
+        for o in range(NB // GROUP):
+            rows = []
+            for b in range(GROUP):
+                at = (o * GROUP + b) * GROUP
+                rows.append(
+                    jnp.where(
+                        keep,
+                        total[at : at + GROUP, side * LANES : (side + 1) * LANES],
+                        0.0,
+                    )
+                )
+            for k in (1, 2, 4):
+                even = (sub & k) == 0
+                rows = [
+                    jnp.where(even, rows[i], rows[i + 1])
+                    + pltpu.roll(jnp.where(even, rows[i + 1], rows[i]), k, 0)
+                    for i in range(0, len(rows), 2)
+                ]
+            octets.append(rows[0])
+        return jnp.concatenate(octets, axis=0)
+
+    def across(off):
+        peer = lax.rem(col + off, ns)
+        return pltpu.make_async_remote_copy(
+            src_ref=tiles.at[peer],
+            dst_ref=part.at[off - 1],
+            send_sem=send1.at[off - 1],
+            recv_sem=recv1.at[off - 1],
+            device_id=(me, peer),
+            device_id_type=MESH,
+        )
+
+    for c in range(comps):
+        look_up(c, me, stage)
+
+        def arrive(off, carry, c=c):
+            exchange(c, off).wait_recv()
+            look_up(c, lax.rem(me - off + n, n), recv)
+            return carry
+
+        lax.fori_loop(1, n, arrive, 0)
+        if c < comps - 1:
+
+            def grams(g, carry, c=c):
+                if c == 0:
+                    acc[g] = gram(g)
+                else:
+                    acc[g] += gram(g)
+                return carry
+
+            lax.fori_loop(0, groups, grams, 0, unroll=2)
+
+    def finish(h):
+        def owner(i, carry):
+            g = i * halves + h
+            total = acc[g] + gram(g)
+            real, imag = diagonal(total, 0), diagonal(total, 1)
+            tiles[2 * h, i] = jnp.where(low, real, pltpu.roll(imag, GROUP // 2, 1))
+            tiles[2 * h + 1, i] = jnp.where(
+                low, pltpu.roll(real, LANES - GROUP // 2, 1), imag
+            )
+            return carry
+
+        lax.fori_loop(0, owners, owner, 0, unroll=2)
+
+    here = col // 2
+    finish(1 - here)
+    for off in range(1, ns):
+
+        @pl.when(lax.rem(col + off, ns) // 2 != here)
+        def _(off=off):
+            across(off).start()
+
+    finish(here)
+    for off in range(1, ns):
+
+        @pl.when(lax.rem(col + off, ns) // 2 == here)
+        def _(off=off):
+            across(off).start()
+
+    for off in range(1, ns):
+        across(off).wait_recv()
+    whole = tiles[col]
+    for off in range(1, ns):
+        whole = whole + part[off - 1]
+    summed[...] = whole
+
+    def along(off):
+        peer = lax.rem(me + off, n)
+        return pltpu.make_async_remote_copy(
+            src_ref=summed.at[peer],
+            dst_ref=last.at[off],
+            send_sem=send2.at[off],
+            recv_sem=recv2.at[off],
+            device_id=(peer, col),
+            device_id_type=MESH,
+        )
+
+    def begin2(off, carry):
+        along(off).start()
+        return carry
+
+    lax.fori_loop(1, n, begin2, 0)
+
+    def add2(off, total):
+        along(off).wait_recv()
+        return total + last[off]
+
+    out[...] = lax.fori_loop(1, n, add2, summed[me])
+
+    for off in range(1, ns):
+        across(off).wait_send()
+
+    def drain(off, carry):
+        for c in range(comps):
+            exchange(c, off).wait_send()
+        along(off).wait_send()
+        return carry
+
+    lax.fori_loop(1, n, drain, 0)
+
+
+def lean_tile(n, ns, bins, weight_scale, snap, table, weights, triads, slots):
+    comps, times, cells = snap.shape
+    owners, per_owner = slots.shape
+    groups = owners * per_owner // GROUP
+    rows = times // NT * 2 * bins
+    vmem = pl.BlockSpec(memory_space=pltpu.VMEM)
+    anywhere = pl.BlockSpec(memory_space=pl.ANY)
+    sem = pltpu.SemaphoreType.DMA
+    return pl.pallas_call(
+        functools.partial(lean_kernel, n, ns, bins, weight_scale),
+        out_shape=jax.ShapeDtypeStruct((NB, LANES), jnp.float32),
+        in_specs=[anywhere, anywhere, vmem, vmem, vmem],
+        out_specs=vmem,
+        scratch_shapes=[
+            pltpu.VMEM((comps, times, cells), jnp.bfloat16),
+            pltpu.VMEM((2, K, NT), jnp.bfloat16),
+            pltpu.VMEM((2 * bins, NT), jnp.bfloat16),
+            pltpu.VMEM((3 * owners * per_owner, bins), jnp.bfloat16),
+            pltpu.VMEM((comps, n, rows, LANES), jnp.bfloat16),
+            pltpu.VMEM((comps, n, rows, LANES), jnp.bfloat16),
+            pltpu.VMEM((3 * owners * per_owner, 4 * LANES), jnp.float32),
+            pltpu.VMEM((groups, NB * GROUP, 2 * LANES), jnp.bfloat16),
+            pltpu.VMEM((groups, 2 * NB * GROUP, 2 * LANES), jnp.bfloat16),
+            pltpu.VMEM((groups, NB * GROUP, 2 * LANES), jnp.float32),
+            pltpu.VMEM((ns, n, NB, LANES), jnp.float32),
+            pltpu.VMEM((ns - 1, n, NB, LANES), jnp.float32),
+            pltpu.VMEM((n, NB, LANES), jnp.float32),
+            pltpu.VMEM((n, NB, LANES), jnp.float32),
+            sem((comps + 1,)),
+            sem((comps, n)),
+            sem((comps, n)),
+            sem((ns - 1,)),
+            sem((ns - 1,)),
+            sem((n,)),
+            sem((n,)),
+        ],
+        compiler_params=pltpu.CompilerParams(
+            collective_id=bins, has_side_effects=True, vmem_limit_bytes=60 * 1024 * 1024
+        ),
+    )(snap, table, weights, triads, slots)
+
+
+def lean(n, ns, snapshots, cell_weights, triads, owner_slots):
+    times, comps, cells = snapshots.shape
+    tile = lean_tile(
+        n,
+        ns,
+        K,
+        1.0 / math.sqrt(comps * cells * ns),
+        snapshots.transpose(1, 0, 2),
+        jnp.asarray(spectral_table().reshape(K, 2, NT).transpose(1, 0, 2)),
+        cell_weights.reshape(n, LANES),
+        triads.T,
+        owner_slots,
+    )
+    mine = owner_slots.shape[1] // ns
+    return tile.reshape(NB, NB, 2, mine).transpose(3, 2, 0, 1).reshape(mine, 2 * NB * NB)
+
+
 def shards(n, ns, snapshots, cell_weights, triads, owner_slots):
     times, comps, cells = snapshots.shape
     owners, slot_count = owner_slots.shape
+    if times % (2 * NT) == 0 and ns == 4 and slot_count == 2 * GROUP and owners == n:
+        return lean(n, ns, snapshots, cell_weights, triads, owner_slots)
     weight_scale = 1.0 / math.sqrt(comps * cells * ns)
     vmem = pl.BlockSpec(memory_space=pltpu.VMEM)
     smem = pl.BlockSpec(memory_space=pltpu.SMEM)

time: 97.4 us -> 89.4 us (0.918)
  local copies, waits for them, and re-layouts: 5.27 us -> 1.59 us
  Pallas kernels: 89.7 us -> 87.5 us
  other arithmetic: 2.14 us -> 0 us
    unnamed x7 -> x0, local copies, waits for them, and re-layouts: 4.27 us -> none
    pallas_call x1, Pallas kernels: 89.7 us -> 87.5 us  [lean_tile(): pl.pallas_call(functools.partial(lean_kernel, n, ns, bins, weight_scale),...]
where the time goes in v1:
time: 89.4 us; the launch traced here: 89.1 us
  Pallas kernels  87.5 us (98%)
  local copies, waits for them, and re-layouts  1.59 us (2%)
    pallas_call x1, Pallas kernels, lean_tile(): pl.pallas_call(functools.partial(lean_kernel, n, ns, bins, weight_scale),...  87.5 us

profile of v1, /device:TPU:0, one launch (start us, length us, event | category | flops | bytes accessed | tf_op | source)
XLA Modules:
  0.0 89.1 jit_solution(12398690990780436851)
XLA Ops:
  0.0 87.5 %shard_map.55 = f32[16,128]{1,0:T(8,128)} custom-call(bf16[3,512,1024]{2,1,0:T(8,128)(2,1)} %bitcast.8, bf16[2,128,256]{2,1,0:T(8,128)(2,1)} %constant.2.clone.table, f32[8,128]{1,0:T(8,128)} %bitcast.10, s32[3,64]{1,0:T(4,128)} %bitcast.11, s32[8,16]{1,0:T(8,128)} %slots.1), custom_call_target="tpu_custom_call" | custom-call | tf_op jit(solution)/shard_map/pallas_call | solution.py:600
  87.6 0.8 copy.8
  88.3 0.1 copy.9
  88.4 0.7 reshape.11

commit v2 on v1

--- a/solution.py
+++ b/solution.py
@@ -15,6 +15,7 @@
 K = 128
 GROUP = 8
 LANES = 128
+BINS = (88, 96, 104, 112, K)
 MESH = pl.DeviceIdType.MESH
 
 
@@ -631,13 +632,31 @@
     )(snap, table, weights, triads, slots)
 
 
+def size_class(bins, triads, out):
+    count = triads.shape[1]
+    freq = lax.broadcasted_iota(jnp.int32, (K, count), 0)
+    hit = (
+        (freq == triads[0:1, :]) | (freq == triads[1:2, :]) | (freq == triads[2:3, :])
+    )
+    used = jnp.sum(jnp.max(jnp.where(hit, 1.0, 0.0), axis=1, keepdims=True))
+    index = jnp.int32(0)
+    for size in bins[:-1]:
+        index += (used > size).astype(jnp.int32)
+    out[0] = index
+
+
 def lean(n, ns, snapshots, cell_weights, triads, owner_slots):
     times, comps, cells = snapshots.shape
-    tile = lean_tile(
-        n,
-        ns,
-        K,
-        1.0 / math.sqrt(comps * cells * ns),
+    index = pl.pallas_call(
+        functools.partial(size_class, BINS),
+        out_shape=jax.ShapeDtypeStruct((1,), jnp.int32),
+        in_specs=[pl.BlockSpec(memory_space=pltpu.VMEM)],
+        out_specs=pl.BlockSpec(memory_space=pltpu.SMEM),
+    )(triads.T)
+    scale = 1.0 / math.sqrt(comps * cells * ns)
+    tile = lax.switch(
+        index[0],
+        [functools.partial(lean_tile, n, ns, bins, scale) for bins in BINS],
         snapshots.transpose(1, 0, 2),
         jnp.asarray(spectral_table().reshape(K, 2, NT).transpose(1, 0, 2)),
         cell_weights.reshape(n, LANES),

time: 89.4 us -> 77.4 us (0.87)
  Pallas kernels: 87.5 us -> 75.6 us
    pallas_call x1, Pallas kernels: 87.5 us -> 74.2 us  [lean_tile(): pl.pallas_call(functools.partial(lean_kernel, n, ns, bins, weight_scale),...]
    pallas_call x0 -> x1, Pallas kernels: none -> 1.41 us  [lean(): pl.pallas_call(functools.partial(size_class, BINS), out_shape=jax.ShapeDt...]
where the time goes in v2:
time: 77.4 us; the launch traced here: 77.2 us
  Pallas kernels  75.6 us (98%)
  local copies, waits for them, and re-layouts  0.89 us (1%)
    pallas_call x1, Pallas kernels, lean_tile(): pl.pallas_call(functools.partial(lean_kernel, n, ns, bins, weight_scale),...  74.2 us

profile of v2, /device:TPU:0, one launch (start us, length us, event | category | flops | bytes accessed | tf_op | source)
XLA Modules:
  0.0 77.2 jit_solution(6308947930251309707)
XLA Ops:
  0.0 1.4 %shard_map.55 = s32[1]{0:T(128)} custom-call(s32[3,64]{1,0:T(4,128)} %bitcast.20), custom_call_target="tpu_custom_call" | custom-call | tf_op jit(solution)/shard_map/pallas_call | solution.py:650
  2.1 74.3 %conditional.1 = (f32[16,128]{1,0:T(8,128)S(1)}) conditional(s32[]{:T(128)} %bitcast.1, (bf16[3,512,1024]{2,1,0:T(8,128)(2,1)}, bf16[2,128,256]{2,1,0:T(8,128)(2,1)}, f32[8,128]{1,0:T(8,128)}, s32[3,64]{1,0:T(4,128)}, s32[8,16]{1,0:T(8,128)}) %tuple.36, (bf16[3,512,1024]{2,1,0:T(8,128)(2,1)}, ...), branch_computations={%region_0.0_spmd, %region_1.0_spmd, %region_2.0_spmd, %region_3.0_... | conditional | bytes 8 | solution.py:657
  2.1 74.2 %branch_2_fun.1 = f32[16,128]{1,0:T(8,128)S(1)} custom-call(bf16[3,512,1024]{2,1,0:T(8,128)(2,1)} %get-tuple-element.71.snap, bf16[2,128,256]{2,1,0:T(8,128)(2,1)} %get-tuple-element.72.table, f32[8,128]{1,0:T(8,128)} %get-tuple-element.73.weights, s32[3,64]{1,0:T(4,128)} %get-tuple-element.74.triads, s32[8,16]{1,0:T(8,128)} %get-tuple-element.75.slots), custom_call_target="tpu_custom_call" | custom-call | tf_op jit(solution)/shard_map/cond/branch_2_fun/pallas_call | solution.py:601
  76.3 0.1 copy.8
  76.4 0.1 copy.9
  76.5 0.7 reshape.14

commit v3 on v2

--- a/solution.py
+++ b/solution.py
@@ -15,7 +15,7 @@
 K = 128
 GROUP = 8
 LANES = 128
-BINS = (88, 96, 104, 112, K)
+BINS = (92, 96, 100, 104, 112, K)
 MESH = pl.DeviceIdType.MESH
 
 
@@ -256,12 +256,15 @@
     weight_scale,
     snap,
     table,
+    weights_at,
+    triads_at,
+    slots_at,
+    out,
+    series,
+    tab,
     weights,
     triads,
     slots,
-    out,
-    series,
-    tab,
     dft,
     pick,
     stage,
@@ -271,16 +274,16 @@
     third,
     acc,
     tiles,
-    part,
-    summed,
-    last,
+    paired,
+    sums,
+    land,
     load_sem,
     send_sem,
     recv_sem,
-    send1,
-    recv1,
-    send2,
-    recv2,
+    send_pair,
+    recv_pair,
+    send_tile,
+    recv_tile,
 ):
     comps, times, cells = series.shape
     blocks = times // NT
@@ -296,28 +299,41 @@
     def iota(shape, axis):
         return lax.broadcasted_iota(jnp.int32, shape, axis)
 
-    fetch_table = pltpu.make_async_copy(table, tab, load_sem.at[comps])
-    fetch_table.start()
+    core, here = lax.rem(col, 2), col // 2
+    sibling = (me, 2 * here + 1 - core)
+    me_at = 2 * me + here
+
+    def chip(off):
+        other = lax.rem(me_at + off, 2 * n)
+        return other // 2, lax.rem(other, 2)
+
+    barrier = pltpu.get_barrier_semaphore()
+
+    def greet(off, carry):
+        i, h = chip(off)
+        pl.semaphore_signal(
+            barrier, inc=1, device_id=(i, 2 * h + core), device_id_type=MESH
+        )
+        return carry
+
+    pl.semaphore_signal(barrier, inc=1, device_id=sibling, device_id_type=MESH)
+    lax.fori_loop(1, 2 * n, greet, 0)
+
+    small = [
+        pltpu.make_async_copy(source, target, load_sem.at[comps + i])
+        for i, (source, target) in enumerate(
+            ((triads_at, triads), (table, tab), (slots_at, slots), (weights_at, weights))
+        )
+    ]
 
     def fetch(c):
         return pltpu.make_async_copy(snap.at[c], series.at[c], load_sem.at[c])
 
+    for copy in small:
+        copy.start()
     for c in range(comps):
         fetch(c).start()
-
-    barrier = pltpu.get_barrier_semaphore()
-
-    def greet(off, carry):
-        pl.semaphore_signal(
-            barrier, inc=1, device_id=(lax.rem(me + off, n), col), device_id_type=MESH
-        )
-        return carry
-
-    lax.fori_loop(1, n, greet, 0)
-    for off in range(1, ns):
-        pl.semaphore_signal(
-            barrier, inc=1, device_id=(me, lax.rem(col + off, ns)), device_id_type=MESH
-        )
+    small[0].wait()
 
     freq = iota((K, count), 0)
     hit = (
@@ -330,7 +346,7 @@
     rank = jnp.dot(below.astype(bf16), used.astype(bf16), preferred_element_type=f32)
     place = jnp.where((rank == column.astype(f32)) & (used > 0.0), 1.0, 0.0)
     chosen = place.T[:bins].astype(bf16)
-    fetch_table.wait()
+    small[1].wait()
     dft[...] = jnp.concatenate(
         [jnp.dot(chosen, tab[r], preferred_element_type=f32) for r in range(2)], axis=0
     ).astype(bf16)
@@ -339,17 +355,21 @@
         fetch(c).wait()
 
         def step(p, carry):
-            for b in range(blocks):
-                y = jnp.dot(
-                    dft[...],
-                    series[
-                        c,
-                        b * NT : (b + 1) * NT,
-                        pl.ds(pl.multiple_of(p * 2 * LANES, 2 * LANES), 2 * LANES),
-                    ],
-                    preferred_element_type=f32,
-                ).astype(bf16)
-                rows = pl.ds(b * 2 * bins, 2 * bins)
+            for pair in range(blocks // 2):
+                y = [
+                    jnp.dot(
+                        dft[...],
+                        series[
+                            c,
+                            b * NT : (b + 1) * NT,
+                            pl.ds(pl.multiple_of(p * 2 * LANES, 2 * LANES), 2 * LANES),
+                        ],
+                        preferred_element_type=f32,
+                    )
+                    for b in (2 * pair, 2 * pair + 1)
+                ]
+                y = jnp.concatenate(y, axis=0).astype(bf16)
+                rows = pl.ds(pair * 4 * bins, 4 * bins)
                 stage[c, 2 * p, rows, :] = y[:, :LANES]
                 stage[c, 2 * p + 1, rows, :] = y[:, LANES:]
             return carry
@@ -368,7 +388,7 @@
         )
 
     transform(0)
-    pl.semaphore_wait(barrier, n - 1 + ns - 1)
+    pl.semaphore_wait(barrier, 2 * n)
     for c in range(comps):
         if c > 0:
             transform(c)
@@ -379,6 +399,10 @@
 
         lax.fori_loop(1, n, begin, 0)
 
+    for copy in small[2:]:
+        copy.wait()
+    width = -(-bins // GROUP) * GROUP
+    shift = width - bins
     wide = (owners, total_slots)
     spread = jnp.where(
         lax.rem(iota((per_owner, total_slots), 1), per_owner)
@@ -405,28 +429,38 @@
             1.0,
             0.0,
         )
-        chosen_all = jnp.dot(
-            place.T.astype(bf16), named.astype(bf16), preferred_element_type=f32
-        )
-        pick[role * total_slots : (role + 1) * total_slots, :] = chosen_all.T[
-            :, :bins
-        ].astype(bf16)
+        for side in range(pick.shape[0]):
+            spot = column.astype(f32) - float(side * shift)
+            at_rank = jnp.where((rank == spot) & (used > 0.0), 1.0, 0.0)
+            chosen_all = jnp.dot(
+                at_rank.T.astype(bf16), named.astype(bf16), preferred_element_type=f32
+            )
+            pick[side, role * total_slots : (role + 1) * total_slots, :] = chosen_all.T[
+                :, :width
+            ].astype(bf16)
 
     w_row = weights[pl.ds(me, 1), :] * weight_scale
 
     def look_up(c, src, ref):
         for pair in range(blocks // 2):
-            sides = []
-            for b in (2 * pair, 2 * pair + 1):
-                both = ref[c, src, b * 2 * bins : (b + 1) * 2 * bins, :]
-                if bins % 16 != 0:
-                    both = both.astype(f32)
-                sides += [both[:bins], both[bins:]]
-            looked[...] = jnp.dot(
-                pick[...],
-                jnp.concatenate(sides, axis=1).astype(bf16),
-                preferred_element_type=f32,
-            )
+            got = ref[c, src, pair * 4 * bins : (pair + 1) * 4 * bins, :]
+            if bins % 16 != 0:
+                got = got.astype(f32)
+            re = [got[b * 2 * bins : b * 2 * bins + width] for b in range(2)]
+            im = [got[(b + 1) * 2 * bins - width : (b + 1) * 2 * bins] for b in range(2)]
+            if shift == 0:
+                looked[...] = jnp.dot(
+                    pick[0],
+                    jnp.concatenate(re + im, axis=1).astype(bf16),
+                    preferred_element_type=f32,
+                )
+            else:
+                for side, values in enumerate((re, im)):
+                    looked[:, side * 2 * LANES : (side + 1) * 2 * LANES] = jnp.dot(
+                        pick[side],
+                        jnp.concatenate(values, axis=1).astype(bf16),
+                        preferred_element_type=f32,
+                    )
             first = src * (blocks * GROUP) + pair * 2 * GROUP
             at = pl.ds(pl.multiple_of(first, 2 * GROUP), 2 * GROUP)
             at_imag = pl.ds(pl.multiple_of(NB * GROUP + first, 2 * GROUP), 2 * GROUP)
@@ -438,12 +472,12 @@
 
                 re, im, c_re, c_im = [], [], [], []
                 for b in range(2):
-                    ar, ai = tile(0, 2 * b), tile(0, 2 * b + 1)
-                    br, bi = tile(1, 2 * b), tile(1, 2 * b + 1)
+                    ar, ai = tile(0, b), tile(0, 2 + b)
+                    br, bi = tile(1, b), tile(1, 2 + b)
                     re.append((ar * br - ai * bi) * w_row)
                     im.append((ar * bi + ai * br) * w_row)
-                    c_re.append(tile(2, 2 * b))
-                    c_im.append(tile(2, 2 * b + 1))
+                    c_re.append(tile(2, b))
+                    c_im.append(tile(2, 2 + b))
                 re, im, c_re, c_im = (
                     jnp.concatenate(v, axis=0) for v in (re, im, c_re, c_im)
                 )
@@ -463,7 +497,7 @@
         )
 
     sub = iota((GROUP, LANES), 0)
-    keep = sub == lax.rem(iota((GROUP, LANES), 1), GROUP)
+    turn = lax.rem(sub - iota((GROUP, LANES), 1) + LANES, GROUP)
     low = lax.rem(iota((NB, LANES), 1), GROUP) < GROUP // 2
 
     def diagonal(total, side):
@@ -472,33 +506,26 @@
             rows = []
             for b in range(GROUP):
                 at = (o * GROUP + b) * GROUP
-                rows.append(
+                rows.append(total[at : at + GROUP, side * LANES : (side + 1) * LANES])
+            for k in (1, 2, 4):
+                even, stay = (sub & k) == 0, (turn & k) == 0
+                rows = [
                     jnp.where(
-                        keep,
-                        total[at : at + GROUP, side * LANES : (side + 1) * LANES],
-                        0.0,
+                        stay,
+                        jnp.where(even, rows[i], rows[i + 1]),
+                        pltpu.roll(jnp.where(even, rows[i + 1], rows[i]), k, 0),
                     )
-                )
-            for k in (1, 2, 4):
-                even = (sub & k) == 0
-                rows = [
-                    jnp.where(even, rows[i], rows[i + 1])
-                    + pltpu.roll(jnp.where(even, rows[i + 1], rows[i]), k, 0)
                     for i in range(0, len(rows), 2)
                 ]
             octets.append(rows[0])
         return jnp.concatenate(octets, axis=0)
 
-    def across(off):
-        peer = lax.rem(col + off, ns)
-        return pltpu.make_async_remote_copy(
-            src_ref=tiles.at[peer],
-            dst_ref=part.at[off - 1],
-            send_sem=send1.at[off - 1],
-            recv_sem=recv1.at[off - 1],
-            device_id=(me, peer),
-            device_id_type=MESH,
-        )
+    def partner(step):
+        total, bit = 0, 1
+        while bit < n:
+            total = total + lax.rem(me // bit + step // bit, 2) * bit
+            bit *= 2
+        return total
 
     for c in range(comps):
         look_up(c, me, stage)
@@ -520,74 +547,96 @@
 
             lax.fori_loop(0, groups, grams, 0, unroll=2)
 
-    def finish(h):
+    def finish(side, h):
         def owner(i, carry):
             g = i * halves + h
             total = acc[g] + gram(g)
             real, imag = diagonal(total, 0), diagonal(total, 1)
-            tiles[2 * h, i] = jnp.where(low, real, pltpu.roll(imag, GROUP // 2, 1))
-            tiles[2 * h + 1, i] = jnp.where(
+            tiles[0, side, i] = jnp.where(low, real, pltpu.roll(imag, GROUP // 2, 1))
+            tiles[1, side, i] = jnp.where(
                 low, pltpu.roll(real, LANES - GROUP // 2, 1), imag
             )
             return carry
 
-        lax.fori_loop(0, owners, owner, 0, unroll=2)
-
-    here = col // 2
-    finish(1 - here)
-    for off in range(1, ns):
-
-        @pl.when(lax.rem(col + off, ns) // 2 != here)
-        def _(off=off):
-            across(off).start()
-
-    finish(here)
-    for off in range(1, ns):
-
-        @pl.when(lax.rem(col + off, ns) // 2 == here)
-        def _(off=off):
-            across(off).start()
-
-    for off in range(1, ns):
-        across(off).wait_recv()
-    whole = tiles[col]
-    for off in range(1, ns):
-        whole = whole + part[off - 1]
-    summed[...] = whole
-
-    def along(off):
-        peer = lax.rem(me + off, n)
+        lax.fori_loop(0, owners, owner, 0, unroll=4)
+
+    def swap(side):
         return pltpu.make_async_remote_copy(
-            src_ref=summed.at[peer],
-            dst_ref=last.at[off],
-            send_sem=send2.at[off],
-            recv_sem=recv2.at[off],
-            device_id=(peer, col),
+            src_ref=tiles.at[1 - core, side],
+            dst_ref=paired.at[side],
+            send_sem=send_pair.at[side],
+            recv_sem=recv_pair.at[side],
+            device_id=sibling,
             device_id_type=MESH,
         )
 
-    def begin2(off, carry):
-        along(off).start()
-        return carry
-
-    lax.fori_loop(1, n, begin2, 0)
-
-    def add2(off, total):
-        along(off).wait_recv()
-        return total + last[off]
-
-    out[...] = lax.fori_loop(1, n, add2, summed[me])
-
-    for off in range(1, ns):
-        across(off).wait_send()
+    def deliver(side, i, h):
+        return pltpu.make_async_remote_copy(
+            src_ref=sums.at[side, i],
+            dst_ref=land.at[me_at],
+            send_sem=send_tile.at[side, i],
+            recv_sem=recv_tile.at[me_at],
+            device_id=(i, 2 * h + core),
+            device_id_type=MESH,
+        )
+
+    for side, h in enumerate((1 - here, here)):
+        finish(side, h)
+        swap(side).start()
+
+    for side, h in enumerate((1 - here, here)):
+        swap(side).wait_recv()
+        chip_sum = tiles[core, side] + paired[side]
+        sums[side] = chip_sum.astype(bf16)
+        if side == 1:
+            paired[side] = chip_sum
+
+        def give(step, carry, side=side, h=h):
+            deliver(side, partner(n - 1 - step), h).start()
+            return carry
+
+        lax.fori_loop(0, n if side == 0 else n - 1, give, 0, unroll=True)
 
     def drain(off, carry):
         for c in range(comps):
             exchange(c, off).wait_send()
-        along(off).wait_send()
         return carry
 
     lax.fori_loop(1, n, drain, 0)
+    for side in range(2):
+        swap(side).wait_send()
+
+    def landed(off):
+        i, h = chip(off)
+        return pltpu.make_async_remote_copy(
+            src_ref=sums.at[0, i],
+            dst_ref=land.at[2 * i + h],
+            send_sem=send_tile.at[0, i],
+            recv_sem=recv_tile.at[2 * i + h],
+            device_id=(i, 2 * h + core),
+            device_id_type=MESH,
+        )
+
+    def collect(off, carry):
+        landed(off).wait_recv()
+        return carry
+
+    lax.fori_loop(1, 2 * n, collect, 0)
+    total = paired[1, me]
+    for off in range(1, 2 * n):
+        total = total + land[lax.rem(me_at + off, 2 * n)].astype(f32)
+    out[...] = total
+
+    def sent(step, carry):
+        deliver(0, step, 1 - here).wait_send()
+        return carry
+
+    def sent_near(off, carry):
+        deliver(1, lax.rem(me + off, n), here).wait_send()
+        return carry
+
+    lax.fori_loop(0, n, sent, 0)
+    lax.fori_loop(1, n, sent_near, 0)
 
 
 def lean_tile(n, ns, bins, weight_scale, snap, table, weights, triads, slots):
@@ -595,36 +644,40 @@
     owners, per_owner = slots.shape
     groups = owners * per_owner // GROUP
     rows = times // NT * 2 * bins
+    width = -(-bins // GROUP) * GROUP
     vmem = pl.BlockSpec(memory_space=pltpu.VMEM)
     anywhere = pl.BlockSpec(memory_space=pl.ANY)
     sem = pltpu.SemaphoreType.DMA
     return pl.pallas_call(
         functools.partial(lean_kernel, n, ns, bins, weight_scale),
         out_shape=jax.ShapeDtypeStruct((NB, LANES), jnp.float32),
-        in_specs=[anywhere, anywhere, vmem, vmem, vmem],
+        in_specs=[anywhere] * 5,
         out_specs=vmem,
         scratch_shapes=[
             pltpu.VMEM((comps, times, cells), jnp.bfloat16),
             pltpu.VMEM((2, K, NT), jnp.bfloat16),
+            pltpu.VMEM(weights.shape, jnp.float32),
+            pltpu.VMEM(triads.shape, jnp.int32),
+            pltpu.VMEM(slots.shape, jnp.int32),
             pltpu.VMEM((2 * bins, NT), jnp.bfloat16),
-            pltpu.VMEM((3 * owners * per_owner, bins), jnp.bfloat16),
+            pltpu.VMEM((1 if width == bins else 2, 3 * owners * per_owner, width), jnp.bfloat16),
             pltpu.VMEM((comps, n, rows, LANES), jnp.bfloat16),
             pltpu.VMEM((comps, n, rows, LANES), jnp.bfloat16),
             pltpu.VMEM((3 * owners * per_owner, 4 * LANES), jnp.float32),
             pltpu.VMEM((groups, NB * GROUP, 2 * LANES), jnp.bfloat16),
             pltpu.VMEM((groups, 2 * NB * GROUP, 2 * LANES), jnp.bfloat16),
             pltpu.VMEM((groups, NB * GROUP, 2 * LANES), jnp.float32),
-            pltpu.VMEM((ns, n, NB, LANES), jnp.float32),
-            pltpu.VMEM((ns - 1, n, NB, LANES), jnp.float32),
-            pltpu.VMEM((n, NB, LANES), jnp.float32),
-            pltpu.VMEM((n, NB, LANES), jnp.float32),
-            sem((comps + 1,)),
+            pltpu.VMEM((2, 2, n, NB, LANES), jnp.float32),
+            pltpu.VMEM((2, n, NB, LANES), jnp.float32),
+            pltpu.VMEM((2, n, NB, LANES), jnp.bfloat16),
+            pltpu.VMEM((2 * n, NB, LANES), jnp.bfloat16),
+            sem((comps + 4,)),
             sem((comps, n)),
             sem((comps, n)),
-            sem((ns - 1,)),
-            sem((ns - 1,)),
-            sem((n,)),
-            sem((n,)),
+            sem((2,)),
+            sem((2,)),
+            sem((2, n)),
+            sem((2 * n,)),
         ],
         compiler_params=pltpu.CompilerParams(
             collective_id=bins, has_side_effects=True, vmem_limit_bytes=60 * 1024 * 1024
@@ -670,7 +723,8 @@
 def shards(n, ns, snapshots, cell_weights, triads, owner_slots):
     times, comps, cells = snapshots.shape
     owners, slot_count = owner_slots.shape
-    if times % (2 * NT) == 0 and ns == 4 and slot_count == 2 * GROUP and owners == n:
+    lean_slots = ns == 4 and slot_count == 2 * GROUP and owners == n
+    if lean_slots and times % (2 * NT) == 0 and n & (n - 1) == 0:
         return lean(n, ns, snapshots, cell_weights, triads, owner_slots)
     weight_scale = 1.0 / math.sqrt(comps * cells * ns)
     vmem = pl.BlockSpec(memory_space=pltpu.VMEM)

time: 77.4 us -> 71.9 us (0.929); the launches traced: 77.2 us -> 70.6 us
  Pallas kernels: 75.6 us -> 68.8 us
    pallas_call x1, Pallas kernels: 74.2 us -> 67.4 us  [lean_tile(): pl.pallas_call(functools.partial(lean_kernel, n, ns, bins, weight_scale),...]
where the time goes in v3:
time: 71.9 us; the launch traced here: 70.6 us
  Pallas kernels  68.8 us (96%)
  local copies, waits for them, and re-layouts  0.89 us (1%)
    pallas_call x1, Pallas kernels, lean_tile(): pl.pallas_call(functools.partial(lean_kernel, n, ns, bins, weight_scale),...  67.4 us

profile of v3, /device:TPU:0, one launch (start us, length us, event | category | flops | bytes accessed | tf_op | source)
XLA Modules:
  0.0 70.6 jit_solution(3342378471175631296)
XLA Ops:
  0.0 1.4 %shard_map.55 = s32[1]{0:T(128)} custom-call(s32[3,64]{1,0:T(4,128)} %bitcast.22), custom_call_target="tpu_custom_call" | custom-call | tf_op jit(solution)/shard_map/pallas_call | solution.py:703
  2.1 67.6 %conditional.1 = (f32[16,128]{1,0:T(8,128)S(1)}) conditional(s32[]{:T(128)} %bitcast.1, (bf16[3,512,1024]{2,1,0:T(8,128)(2,1)}, bf16[2,128,256]{2,1,0:T(8,128)(2,1)}, f32[8,128]{1,0:T(8,128)}, s32[3,64]{1,0:T(4,128)}, s32[8,16]{1,0:T(8,128)}) %tuple.42, (bf16[3,512,1024]{2,1,0:T(8,128)(2,1)}, ...), branch_computations={%region_0.0_spmd, %region_1.0_spmd, %region_2.0_spmd, %region_3.0_... | conditional | bytes 8 | solution.py:710
  2.1 67.4 %branch_1_fun.1 = f32[16,128]{1,0:T(8,128)S(1)} custom-call(bf16[3,512,1024]{2,1,0:T(8,128)(2,1)} %get-tuple-element.77.snap, bf16[2,128,256]{2,1,0:T(8,128)(2,1)} %get-tuple-element.78.table, f32[8,128]{1,0:T(8,128)} %get-tuple-element.79.weights_at, s32[3,64]{1,0:T(4,128)} %get-tuple-element.80.triads_at, s32[8,16]{1,0:T(8,128)} %get-tuple-element.81.slots_at), custom_call_target="tpu_custom_call" | custom-call | tf_op jit(solution)/shard_map/cond/branch_1_fun/pallas_call | solution.py:651
  69.7 0.1 copy.8
  69.8 0.1 copy.9
  69.9 0.7 reshape.14

commit v4 on v3

--- a/solution.py
+++ b/solution.py
@@ -423,6 +423,7 @@
     slot_freq = jnp.dot(
         (triads[...] + 1).astype(f32).astype(bf16), holds, preferred_element_type=f32
     )
+    found = [[], []]
     for role in range(3):
         named = jnp.where(
             iota((K, total_slots), 0).astype(f32) + 1.0 == slot_freq[role : role + 1, :],
@@ -435,9 +436,16 @@
             chosen_all = jnp.dot(
                 at_rank.T.astype(bf16), named.astype(bf16), preferred_element_type=f32
             )
-            pick[side, role * total_slots : (role + 1) * total_slots, :] = chosen_all.T[
-                :, :width
-            ].astype(bf16)
+            found[side].append(chosen_all.T[:, :width])
+    for side in range(pick.shape[0]):
+        pick[side] = jnp.concatenate(
+            [
+                found[side][role][g * GROUP : (g + 1) * GROUP]
+                for g in range(groups)
+                for role in range(3)
+            ],
+            axis=0,
+        ).astype(bf16)
 
     w_row = weights[pl.ds(me, 1), :] * weight_scale
 
@@ -467,7 +475,7 @@
 
             def group(g, carry):
                 def tile(role, q):
-                    row = pl.multiple_of(role * total_slots + g * GROUP, GROUP)
+                    row = pl.multiple_of((3 * g + role) * GROUP, GROUP)
                     return looked[pl.ds(row, GROUP), q * LANES : (q + 1) * LANES]
 
                 re, im, c_re, c_im = [], [], [], []
@@ -489,7 +497,7 @@
                 third[g, at_imag, LANES:] = (-c_re).astype(bf16)
                 return carry
 
-            lax.fori_loop(0, groups, group, 0, unroll=4)
+            lax.fori_loop(0, groups, group, 0, unroll=True)
 
     def gram(g):
         return lax.dot_general(
@@ -527,6 +535,28 @@
             bit *= 2
         return total
 
+    half = owners // 2
+
+    def fold(side, first, past, with_acc, with_tiles):
+        def tile(at, carry):
+            i, h = partner(n - 1 - side * half - at // 2), lax.rem(at, 2)
+            g = i * halves + h
+            total = acc[g] + gram(g) if with_acc else gram(g)
+            real, imag = diagonal(total, 0), diagonal(total, 1)
+            both = (
+                jnp.where(low, real, pltpu.roll(imag, GROUP // 2, 1)),
+                jnp.where(low, pltpu.roll(real, LANES - GROUP // 2, 1), imag),
+            )
+            for q in range(2):
+                before = tiles[q, side, at] if with_tiles else 0.0
+                tiles[q, side, at] = before + both[q]
+            return carry
+
+        lax.fori_loop(first, past, tile, 0, unroll=True)
+
+    def finish(side, first, past):
+        fold(side, first, past, False, comps > 1)
+
     for c in range(comps):
         look_up(c, me, stage)
 
@@ -536,29 +566,16 @@
             return carry
 
         lax.fori_loop(1, n, arrive, 0)
-        if c < comps - 1:
+        if c < comps - 2:
 
             def grams(g, carry, c=c):
-                if c == 0:
-                    acc[g] = gram(g)
-                else:
-                    acc[g] += gram(g)
+                acc[g] = gram(g) if c == 0 else acc[g] + gram(g)
                 return carry
 
             lax.fori_loop(0, groups, grams, 0, unroll=2)
-
-    def finish(side, h):
-        def owner(i, carry):
-            g = i * halves + h
-            total = acc[g] + gram(g)
-            real, imag = diagonal(total, 0), diagonal(total, 1)
-            tiles[0, side, i] = jnp.where(low, real, pltpu.roll(imag, GROUP // 2, 1))
-            tiles[1, side, i] = jnp.where(
-                low, pltpu.roll(real, LANES - GROUP // 2, 1), imag
-            )
-            return carry
-
-        lax.fori_loop(0, owners, owner, 0, unroll=4)
+        elif c == comps - 2:
+            for side in range(2):
+                fold(side, 0, n, c > 0, False)
 
     def swap(side):
         return pltpu.make_async_remote_copy(
@@ -570,32 +587,34 @@
             device_id_type=MESH,
         )
 
-    def deliver(side, i, h):
+    def deliver(side, step, h):
         return pltpu.make_async_remote_copy(
-            src_ref=sums.at[side, i],
+            src_ref=sums.at[side, 2 * step + h],
             dst_ref=land.at[me_at],
-            send_sem=send_tile.at[side, i],
+            send_sem=send_tile.at[side, 2 * step + h],
             recv_sem=recv_tile.at[me_at],
-            device_id=(i, 2 * h + core),
+            device_id=(partner(n - 1 - side * half - step), 2 * h + core),
             device_id_type=MESH,
         )
 
-    for side, h in enumerate((1 - here, here)):
-        finish(side, h)
-        swap(side).start()
-
-    for side, h in enumerate((1 - here, here)):
+    def pass_on(side):
         swap(side).wait_recv()
         chip_sum = tiles[core, side] + paired[side]
         sums[side] = chip_sum.astype(bf16)
         if side == 1:
             paired[side] = chip_sum
-
-        def give(step, carry, side=side, h=h):
-            deliver(side, partner(n - 1 - step), h).start()
-            return carry
-
-        lax.fori_loop(0, n if side == 0 else n - 1, give, 0, unroll=True)
+        for step in range(half):
+            deliver(side, step, 1 - here).start()
+            if side * half + step < n - 1:
+                deliver(side, step, here).start()
+
+    finish(0, 0, n)
+    swap(0).start()
+    finish(1, 0, 4)
+    pass_on(0)
+    finish(1, 4, n)
+    swap(1).start()
+    pass_on(1)
 
     def drain(off, carry):
         for c in range(comps):
@@ -609,9 +628,9 @@
     def landed(off):
         i, h = chip(off)
         return pltpu.make_async_remote_copy(
-            src_ref=sums.at[0, i],
+            src_ref=sums.at[0, 0],
             dst_ref=land.at[2 * i + h],
-            send_sem=send_tile.at[0, i],
+            send_sem=send_tile.at[0, 0],
             recv_sem=recv_tile.at[2 * i + h],
             device_id=(i, 2 * h + core),
             device_id_type=MESH,
@@ -622,21 +641,16 @@
         return carry
 
     lax.fori_loop(1, 2 * n, collect, 0)
-    total = paired[1, me]
+    total = paired[1, n - 2 + here]
     for off in range(1, 2 * n):
         total = total + land[lax.rem(me_at + off, 2 * n)].astype(f32)
     out[...] = total
 
-    def sent(step, carry):
-        deliver(0, step, 1 - here).wait_send()
-        return carry
-
-    def sent_near(off, carry):
-        deliver(1, lax.rem(me + off, n), here).wait_send()
-        return carry
-
-    lax.fori_loop(0, n, sent, 0)
-    lax.fori_loop(1, n, sent_near, 0)
+    for side in range(2):
+        for step in range(half):
+            deliver(side, step, 1 - here).wait_send()
+            if side * half + step < n - 1:
+                deliver(side, step, here).wait_send()
 
 
 def lean_tile(n, ns, bins, weight_scale, snap, table, weights, triads, slots):

time: 71.9 us -> 69.8 us (0.971); the launches traced: 70.6 us -> 69.6 us
  Pallas kernels: 68.8 us -> 67.8 us
    pallas_call x1, Pallas kernels: 67.4 us -> 66.4 us  [lean_tile(): pl.pallas_call(functools.partial(lean_kernel, n, ns, bins, weight_scale),...]
where the time goes in v4:
time: 69.8 us; the launch traced here: 69.6 us
  Pallas kernels  67.8 us (97%)
  local copies, waits for them, and re-layouts  0.89 us (1%)
    pallas_call x1, Pallas kernels, lean_tile(): pl.pallas_call(functools.partial(lean_kernel, n, ns, bins, weight_scale),...  66.4 us
    pallas_call x1, Pallas kernels, lean(): pl.pallas_call(functools.partial(size_class, BINS), out_shape=jax.ShapeDt...  1.42 us

profile of v4, /device:TPU:0, one launch (start us, length us, event | category | flops | bytes accessed | tf_op | source)
XLA Modules:
  0.0 69.6 jit_solution(926718580949563580)
XLA Ops:
  0.0 1.4 %shard_map.55 = s32[1]{0:T(128)} custom-call(s32[3,64]{1,0:T(4,128)} %bitcast.22), custom_call_target="tpu_custom_call" | custom-call | tf_op jit(solution)/shard_map/pallas_call | solution.py:717
  2.1 66.7 %conditional.1 = (f32[16,128]{1,0:T(8,128)S(1)}) conditional(s32[]{:T(128)} %bitcast.1, (bf16[3,512,1024]{2,1,0:T(8,128)(2,1)}, bf16[2,128,256]{2,1,0:T(8,128)(2,1)}, f32[8,128]{1,0:T(8,128)}, s32[3,64]{1,0:T(4,128)}, s32[8,16]{1,0:T(8,128)}) %tuple.42, (bf16[3,512,1024]{2,1,0:T(8,128)(2,1)}, ...), branch_computations={%region_0.0_spmd, %region_1.0_spmd, %region_2.0_spmd, %region_3.0_... | conditional | bytes 8 | solution.py:724
  2.1 66.4 %branch_1_fun.1 = f32[16,128]{1,0:T(8,128)S(1)} custom-call(bf16[3,512,1024]{2,1,0:T(8,128)(2,1)} %get-tuple-element.77.snap, bf16[2,128,256]{2,1,0:T(8,128)(2,1)} %get-tuple-element.78.table, f32[8,128]{1,0:T(8,128)} %get-tuple-element.79.weights_at, s32[3,64]{1,0:T(4,128)} %get-tuple-element.80.triads_at, s32[8,16]{1,0:T(8,128)} %get-tuple-element.81.slots_at), custom_call_target="tpu_custom_call" | custom-call | tf_op jit(solution)/shard_map/cond/branch_1_fun/pallas_call | solution.py:665
  68.7 0.1 copy.8
  68.8 0.1 copy.9
  68.9 0.7 %reshape.14 = f32[4,512]{1,0:T(4,128)} reshape(f32[4,2,16,16]{3,2,1,0:T(8,128)S(1)} %copy.9) | data formatting | bytes 16384 | tf_op jit(solution)/shard_map/reshape | solution.py:734

commit v5 on v4

--- a/solution.py
+++ b/solution.py
@@ -15,7 +15,7 @@
 K = 128
 GROUP = 8
 LANES = 128
-BINS = (92, 96, 100, 104, 112, K)
+BINS = (92, 94, 96, 98, 100, 102, 104, 108, K)
 MESH = pl.DeviceIdType.MESH
 
 
@@ -247,6 +247,15 @@
         return carry
 
     lax.fori_loop(1, n, drain, 0)
+
+
+def windows(bins):
+    starts = [q * bins // GROUP * GROUP for q in range(4)]
+    width = max(
+        -(-(q * bins - start + bins) // GROUP) * GROUP for q, start in enumerate(starts)
+    )
+    starts = [min(start, 4 * bins - width) for start in starts]
+    return width, starts, [q * bins - start for q, start in enumerate(starts)]
 
 
 def lean_kernel(
@@ -286,7 +295,6 @@
     recv_tile,
 ):
     comps, times, cells = series.shape
-    blocks = times // NT
     count = triads.shape[1]
     owners, per_owner = slots.shape
     total_slots = owners * per_owner
@@ -344,34 +352,44 @@
     column = iota((K, K), 1)
     below = jnp.where(column < iota((K, K), 0), 1.0, 0.0)
     rank = jnp.dot(below.astype(bf16), used.astype(bf16), preferred_element_type=f32)
-    place = jnp.where((rank == column.astype(f32)) & (used > 0.0), 1.0, 0.0)
-    chosen = place.T[:bins].astype(bf16)
+    rank_row, used_row = rank.T[0:1], used.T[0:1]
     small[1].wait()
-    dft[...] = jnp.concatenate(
-        [jnp.dot(chosen, tab[r], preferred_element_type=f32) for r in range(2)], axis=0
-    ).astype(bf16)
+    late = 2 * bins % GROUP
+    for b in range(2):
+        at = iota((dft.shape[1], K), 0).astype(f32) - float(b * late)
+        halves_of = [
+            jnp.where((at - float(r * bins) == rank_row) & (used_row > 0.0), 1.0, 0.0)
+            for r in range(2)
+        ]
+        dft[b] = sum(
+            jnp.dot(pick_rows.astype(bf16), tab[r], preferred_element_type=f32)
+            for r, pick_rows in enumerate(halves_of)
+        ).astype(bf16)
 
     def transform(c):
         fetch(c).wait()
 
         def step(p, carry):
-            for pair in range(blocks // 2):
-                y = [
-                    jnp.dot(
-                        dft[...],
-                        series[
-                            c,
-                            b * NT : (b + 1) * NT,
-                            pl.ds(pl.multiple_of(p * 2 * LANES, 2 * LANES), 2 * LANES),
-                        ],
-                        preferred_element_type=f32,
-                    )
-                    for b in (2 * pair, 2 * pair + 1)
-                ]
-                y = jnp.concatenate(y, axis=0).astype(bf16)
-                rows = pl.ds(pair * 4 * bins, 4 * bins)
-                stage[c, 2 * p, rows, :] = y[:, :LANES]
-                stage[c, 2 * p + 1, rows, :] = y[:, LANES:]
+            first, second = [
+                jnp.dot(
+                    dft[b],
+                    series[
+                        c,
+                        b * NT : (b + 1) * NT,
+                        pl.ds(pl.multiple_of(p * 2 * LANES, 2 * LANES), 2 * LANES),
+                    ],
+                    preferred_element_type=f32,
+                )
+                for b in range(2)
+            ]
+            if late == 0:
+                pieces = [first, second]
+            else:
+                end = 2 * bins - late
+                pieces = [first[:end], first[end:] + second[:GROUP], second[GROUP:]]
+            y = jnp.concatenate(pieces, axis=0).astype(bf16)
+            stage[c, 2 * p] = y[:, :LANES]
+            stage[c, 2 * p + 1] = y[:, LANES:]
             return carry
 
         lax.fori_loop(0, n // 2, step, 0)
@@ -401,8 +419,8 @@
 
     for copy in small[2:]:
         copy.wait()
-    width = -(-bins // GROUP) * GROUP
-    shift = width - bins
+    width, starts, shifts = windows(bins)
+    kinds = sorted(set(shifts))
     wide = (owners, total_slots)
     spread = jnp.where(
         lax.rem(iota((per_owner, total_slots), 1), per_owner)
@@ -423,21 +441,21 @@
     slot_freq = jnp.dot(
         (triads[...] + 1).astype(f32).astype(bf16), holds, preferred_element_type=f32
     )
-    found = [[], []]
+    found = [[] for _ in kinds]
     for role in range(3):
         named = jnp.where(
             iota((K, total_slots), 0).astype(f32) + 1.0 == slot_freq[role : role + 1, :],
             1.0,
             0.0,
         )
-        for side in range(pick.shape[0]):
-            spot = column.astype(f32) - float(side * shift)
+        for side, shift in enumerate(kinds):
+            spot = column.astype(f32) - float(shift)
             at_rank = jnp.where((rank == spot) & (used > 0.0), 1.0, 0.0)
             chosen_all = jnp.dot(
                 at_rank.T.astype(bf16), named.astype(bf16), preferred_element_type=f32
             )
             found[side].append(chosen_all.T[:, :width])
-    for side in range(pick.shape[0]):
+    for side in range(len(kinds)):
         pick[side] = jnp.concatenate(
             [
                 found[side][role][g * GROUP : (g + 1) * GROUP]
@@ -450,54 +468,49 @@
     w_row = weights[pl.ds(me, 1), :] * weight_scale
 
     def look_up(c, src, ref):
-        for pair in range(blocks // 2):
-            got = ref[c, src, pair * 4 * bins : (pair + 1) * 4 * bins, :]
-            if bins % 16 != 0:
-                got = got.astype(f32)
-            re = [got[b * 2 * bins : b * 2 * bins + width] for b in range(2)]
-            im = [got[(b + 1) * 2 * bins - width : (b + 1) * 2 * bins] for b in range(2)]
-            if shift == 0:
-                looked[...] = jnp.dot(
-                    pick[0],
-                    jnp.concatenate(re + im, axis=1).astype(bf16),
-                    preferred_element_type=f32,
-                )
-            else:
-                for side, values in enumerate((re, im)):
-                    looked[:, side * 2 * LANES : (side + 1) * 2 * LANES] = jnp.dot(
-                        pick[side],
-                        jnp.concatenate(values, axis=1).astype(bf16),
-                        preferred_element_type=f32,
-                    )
-            first = src * (blocks * GROUP) + pair * 2 * GROUP
-            at = pl.ds(pl.multiple_of(first, 2 * GROUP), 2 * GROUP)
-            at_imag = pl.ds(pl.multiple_of(NB * GROUP + first, 2 * GROUP), 2 * GROUP)
-
-            def group(g, carry):
-                def tile(role, q):
-                    row = pl.multiple_of((3 * g + role) * GROUP, GROUP)
-                    return looked[pl.ds(row, GROUP), q * LANES : (q + 1) * LANES]
-
-                re, im, c_re, c_im = [], [], [], []
-                for b in range(2):
-                    ar, ai = tile(0, b), tile(0, 2 + b)
-                    br, bi = tile(1, b), tile(1, 2 + b)
-                    re.append((ar * br - ai * bi) * w_row)
-                    im.append((ar * bi + ai * br) * w_row)
-                    c_re.append(tile(2, b))
-                    c_im.append(tile(2, 2 + b))
-                re, im, c_re, c_im = (
-                    jnp.concatenate(v, axis=0) for v in (re, im, c_re, c_im)
-                )
-                prod[g, at, :LANES] = re.astype(bf16)
-                prod[g, at, LANES:] = im.astype(bf16)
-                third[g, at, :LANES] = c_re.astype(bf16)
-                third[g, at, LANES:] = c_im.astype(bf16)
-                third[g, at_imag, :LANES] = c_im.astype(bf16)
-                third[g, at_imag, LANES:] = (-c_re).astype(bf16)
-                return carry
-
-            lax.fori_loop(0, groups, group, 0, unroll=True)
+        got = ref[c, src].astype(f32)
+        for side, shift in enumerate(kinds):
+            parts = [q for q in range(4) if shifts[q] == shift]
+            values = [got[starts[q] : starts[q] + width] for q in parts]
+            rows = jnp.dot(
+                pick[side],
+                jnp.concatenate(values, axis=1).astype(bf16),
+                preferred_element_type=f32,
+            )
+            for i, q in enumerate(parts):
+                looked[:, q * LANES : (q + 1) * LANES] = rows[
+                    :, i * LANES : (i + 1) * LANES
+                ]
+        at = pl.ds(pl.multiple_of(src * 2 * GROUP, 2 * GROUP), 2 * GROUP)
+        at_imag = pl.ds(
+            pl.multiple_of((NB + 2 * src) * GROUP, 2 * GROUP), 2 * GROUP
+        )
+
+        def group(g, carry):
+            def tile(role, q):
+                row = pl.multiple_of((3 * g + role) * GROUP, GROUP)
+                return looked[pl.ds(row, GROUP), q * LANES : (q + 1) * LANES]
+
+            re, im, c_re, c_im = [], [], [], []
+            for b in range(2):
+                ar, ai = tile(0, 2 * b), tile(0, 2 * b + 1)
+                br, bi = tile(1, 2 * b), tile(1, 2 * b + 1)
+                re.append((ar * br - ai * bi) * w_row)
+                im.append((ar * bi + ai * br) * w_row)
+                c_re.append(tile(2, 2 * b))
+                c_im.append(tile(2, 2 * b + 1))
+            re, im, c_re, c_im = (
+                jnp.concatenate(v, axis=0) for v in (re, im, c_re, c_im)
+            )
+            prod[g, at, :LANES] = re.astype(bf16)
+            prod[g, at, LANES:] = im.astype(bf16)
+            third[g, at, :LANES] = c_re.astype(bf16)
+            third[g, at, LANES:] = c_im.astype(bf16)
+            third[g, at_imag, :LANES] = c_im.astype(bf16)
+            third[g, at_imag, LANES:] = (-c_re).astype(bf16)
+            return carry
+
+        lax.fori_loop(0, groups, group, 0, unroll=True)
 
     def gram(g):
         return lax.dot_general(
@@ -657,8 +670,8 @@
     comps, times, cells = snap.shape
     owners, per_owner = slots.shape
     groups = owners * per_owner // GROUP
-    rows = times // NT * 2 * bins
-    width = -(-bins // GROUP) * GROUP
+    rows = 4 * bins
+    width, _, shifts = windows(bins)
     vmem = pl.BlockSpec(memory_space=pltpu.VMEM)
     anywhere = pl.BlockSpec(memory_space=pl.ANY)
     sem = pltpu.SemaphoreType.DMA
@@ -673,8 +686,8 @@
             pltpu.VMEM(weights.shape, jnp.float32),
             pltpu.VMEM(triads.shape, jnp.int32),
             pltpu.VMEM(slots.shape, jnp.int32),
-            pltpu.VMEM((2 * bins, NT), jnp.bfloat16),
-            pltpu.VMEM((1 if width == bins else 2, 3 * owners * per_owner, width), jnp.bfloat16),
+            pltpu.VMEM((2, -(-2 * bins // GROUP) * GROUP, NT), jnp.bfloat16),
+            pltpu.VMEM((len(set(shifts)), 3 * owners * per_owner, width), jnp.bfloat16),
             pltpu.VMEM((comps, n, rows, LANES), jnp.bfloat16),
             pltpu.VMEM((comps, n, rows, LANES), jnp.bfloat16),
             pltpu.VMEM((3 * owners * per_owner, 4 * LANES), jnp.float32),
@@ -738,7 +751,7 @@
     times, comps, cells = snapshots.shape
     owners, slot_count = owner_slots.shape
     lean_slots = ns == 4 and slot_count == 2 * GROUP and owners == n
-    if lean_slots and times % (2 * NT) == 0 and n & (n - 1) == 0:
+    if lean_slots and times == 2 * NT and n & (n - 1) == 0:
         return lean(n, ns, snapshots, cell_weights, triads, owner_slots)
     weight_scale = 1.0 / math.sqrt(comps * cells * ns)
     vmem = pl.BlockSpec(memory_space=pltpu.VMEM)

time: 69.8 us -> 71.8 us (1.029)
  Pallas kernels: 67.8 us -> 68.9 us
    pallas_call x1, Pallas kernels: 66.4 us -> 67.5 us  [lean_tile(): pl.pallas_call(functools.partial(lean_kernel, n, ns, bins, weight_scale),...]
where the time goes in v5:
time: 71.8 us; the launch traced here: 71.2 us
  Pallas kernels  68.9 us (96%)
  local copies, waits for them, and re-layouts  0.89 us (1%)
  loops' own time  0.75 us (1%)
    pallas_call x1, Pallas kernels, lean_tile(): pl.pallas_call(functools.partial(lean_kernel, n, ns, bins, weight_scale),...  67.5 us

profile of v5, /device:TPU:0, one launch (start us, length us, event | category | flops | bytes accessed | tf_op | source)
XLA Modules:
  0.0 71.2 jit_solution(8901853476428518685)
XLA Ops:
  0.0 1.4 %shard_map.55 = s32[1]{0:T(128)} custom-call(s32[3,64]{1,0:T(4,128)} %bitcast.28), custom_call_target="tpu_custom_call" | custom-call | tf_op jit(solution)/shard_map/pallas_call | solution.py:730
  2.1 68.2 %conditional.1 = (f32[16,128]{1,0:T(8,128)S(1)}) conditional(s32[]{:T(128)} %bitcast.1, (bf16[3,512,1024]{2,1,0:T(8,128)(2,1)}, bf16[2,128,256]{2,1,0:T(8,128)(2,1)}, f32[8,128]{1,0:T(8,128)}, s32[3,64]{1,0:T(4,128)}, s32[8,16]{1,0:T(8,128)}) %tuple.60, (bf16[3,512,1024]{2,1,0:T(8,128)(2,1)}, ...), branch_computations={%region_0.0_spmd, %region_1.0_spmd, %region_2.0_spmd, %region_3.0_... | conditional | bytes 8 | solution.py:737
  2.3 67.5 %branch_3_fun.1 = f32[16,128]{1,0:T(8,128)S(1)} custom-call(bf16[3,512,1024]{2,1,0:T(8,128)(2,1)} %get-tuple-element.120.snap, bf16[2,128,256]{2,1,0:T(8,128)(2,1)} %get-tuple-element.121.table, f32[8,128]{1,0:T(8,128)} %get-tuple-element.122.weights_at, s32[3,64]{1,0:T(4,128)} %get-tuple-element.123.triads_at, s32[8,16]{1,0:T(8,128)} %get-tuple-element.124.slots_at), custom_call_target="tpu_custom_call" | custom-call | tf_op jit(solution)/shard_map/cond/branch_3_fun/pallas_call | solution.py:678
  70.3 0.1 copy.8
  70.4 0.1 copy.9
  70.5 0.7 reshape.14
